TPU v7x, 512 devices: a whole 4x8x8 slice. The times are simulated.
512 devices in a mesh: dp: 64 (over z, x, core), tensor: 8 (over y).
Axes of the slice: x: 4, y: 8, z: 8, core: 2. Of those that a mesh axis runs over, the one named last changes fastest.
Arguments:
- activations: bfloat16 [64, 2048, 320], P('dp'), may hold values from -6 to 6
- cotangent: bfloat16 [64, 128, 13824], P('dp', None, 'tensor'), may hold values from -3 to 3
- weight: bfloat16 [5120, 13824], P('dp', 'tensor'), may hold values from -0.078125 to 0.078125
- error_buffer: bfloat16 [64, 320, 13824], P('dp', None, 'tensor'), may hold values from -32 to 32
- warm_factor: float32 [13824, 32], P('tensor'), may hold values from -6 to 6
Outputs:
- input_gradient: bfloat16 [64, 2048, 320], P('dp', 'tensor')
- error_next: bfloat16 [64, 320, 13824], P('dp', None, 'tensor')
- update: bfloat16 [5120, 13824], P('dp', 'tensor')
All inputs are finite; a program needn't handle non-finite values.
Results may differ from a plain program's by a relative error of at most 0.0012.
Values may be sent and summed in bfloat16 or wider, within the bound.
A program may use at most 64 MiB of HBM per device.

v0:
```python
import jax
import jax.numpy as jnp
from jax import lax
from jax.sharding import PartitionSpec as P

GROUP = 16


HIGHEST_PRECISION = lax.Precision.HIGHEST


def partner_2(value, axis, stride):
    return lax.ppermute(value, axis, [(i, i ^ 1 << stride) for i in range(lax.axis_size(axis))])


def join_pair(own_block, partner_block, position, bit_index):
    upper_half = position // 2**bit_index % 2 == 1
    return jnp.where(
        upper_half,
        jnp.concatenate([partner_block, own_block], 0),
        jnp.concatenate([own_block, partner_block], 0),
    )


def body(activations, cotangent, weight, error_buffer, warm_factor):
    devices = lax.axis_size("dp")
    replicas = devices // GROUP
    low_bits = replicas.bit_length() - 1
    all_bits = devices.bit_length() - 1
    position = lax.axis_index("dp")
    group_slot = position // replicas
    replica_slot = position % replicas
    tokens = activations[0]
    weight_slab = weight
    for bit_index in range(low_bits):
        partner = partner_2(weight_slab, "dp", bit_index)
        weight_slab = join_pair(weight_slab, partner, position, bit_index)
    upstream = cotangent[0]
    for bit_index in range(low_bits, all_bits):
        partner = partner_2(upstream, "dp", bit_index)
        upstream = join_pair(upstream, partner, position, bit_index)
    gradient = lax.dot_general(
        tokens, upstream, (((0,), (0,)), ((), ())), preferred_element_type=jnp.float32
    )
    merged = error_buffer[0].astype(jnp.float32) + gradient
    input_part = lax.psum_scatter(
        lax.dot_general(
            upstream, weight_slab, (((1,), (1,)), ((), ())), preferred_element_type=jnp.float32
        ),
        "tensor",
        scatter_dimension=0,
        tiled=True,
    )
    projected = jnp.dot(merged, warm_factor, precision=HIGHEST_PRECISION)
    selector = (jnp.arange(GROUP) == group_slot).astype(jnp.float32)
    padded = (selector[:, None, None] * projected[None]).reshape(-1, projected.shape[1])
    whole_factor = lax.psum(padded, "dp")
    gram_matrix = jnp.dot(whole_factor.T, whole_factor, precision=HIGHEST_PRECISION)
    own_rows = lax.dynamic_slice_in_dim(
        whole_factor, group_slot * projected.shape[0], projected.shape[0], 0
    )
    triangle = jnp.linalg.cholesky(gram_matrix)
    orthonormal_rows = jax.scipy.linalg.solve_triangular(triangle, own_rows.T, lower=True).T
    local_second = lax.dot_general(
        merged,
        orthonormal_rows,
        (((0,), (0,)), ((), ())),
        precision=HIGHEST_PRECISION,
        preferred_element_type=jnp.float32,
    )
    second_factor = lax.psum(local_second, "dp") / replicas
    approximation = jnp.dot(orthonormal_rows, second_factor.T, precision=HIGHEST_PRECISION)
    error_next = (merged - approximation).astype(jnp.bfloat16)[None]
    update = lax.dynamic_slice_in_dim(
        approximation, replica_slot * weight.shape[0], weight.shape[0], 0
    ).astype(jnp.bfloat16)
    return (input_part.astype(jnp.bfloat16)[None], error_next, update)


def solution(mesh):
    in_specs = (
        P("dp", None, None),
        P("dp", None, "tensor"),
        P("dp", "tensor"),
        P("dp", None, "tensor"),
        P("tensor", None),
    )
    out_specs = (P("dp", "tensor", None), P("dp", None, "tensor"), P("dp", "tensor"))
    return jax.shard_map(body, mesh=mesh, in_specs=in_specs, out_specs=out_specs, check_vma=False)
```

profile of v0, /device:TPU:40, one launch (start us, length us, event | category | flops | bytes accessed | tf_op | source)
XLA Modules:
  0.0 731.4 jit_solution(3267048852908502387)
XLA Ops:
  8.0 0.0 copy-start
  8.0 0.0 all-reduce.3.cloned.1.call-start
  8.1 5.1 collective-permute-start
  13.2 10.5 %collective-permute-done = bf16[128,1728]{0,1:T(8,128)(2,1)S(1)} collective-permute-done((bf16[128,1728]{0,1:T(8,128)(2,1)}, bf16[128,1728]{0,1:T(8,128)(2,1)S(1)}, u32[]{:S(2)}, u32[]{:S(2)}) %collective-permute-start) | collective-permute-done | bytes 442400 | tf_op jit(solution)/shard_map/ppermute | solution.py:13
  23.7 1.4 maximum_select_fusion.7
  25.1 0.0 copy-start.3
  25.2 4.3 collective-permute-start.1
  29.5 18.8 %collective-permute-done.1 = bf16[256,1728]{0,1:T(8,128)(2,1)} collective-permute-done((bf16[256,1728]{0,1:T(8,128)(2,1)S(1)}, bf16[256,1728]{0,1:T(8,128)(2,1)}, u32[]{:S(2)}, u32[]{:S(2)}) %collective-permute-start.1) | collective-permute-done | bytes 884768 | tf_op jit(solution)/shard_map/ppermute | solution.py:13
  48.3 2.5 maximum_select_fusion.2
  50.8 6.1 collective-permute-start.2
  56.9 0.0 copy-start.4
  56.9 75.1 %collective-permute-done.2 = bf16[512,1728]{0,1:T(8,128)(2,1)} collective-permute-done((bf16[512,1728]{0,1:T(8,128)(2,1)S(1)}, bf16[512,1728]{0,1:T(8,128)(2,1)}, u32[]{:S(2)}, u32[]{:S(2)}) %collective-permute-start.2) | collective-permute-done | bytes 1769504 | tf_op jit(solution)/shard_map/ppermute | solution.py:13
  132.0 4.3 maximum_select_fusion.1
  136.3 8.4 %collective-permute-start.3 = (bf16[1024,1728]{0,1:T(8,128)(2,1)}, bf16[1024,1728]{0,1:T(8,128)(2,1)}, u32[]{:S(2)}, u32[]{:S(2)}) collective-permute-start(bf16[1024,1728]{0,1:T(8,128)(2,1)} %maximum_select_fusion.1), channel_id=1, source_target_pairs={{0,256},{8,264},{16,272},{24,280},{32,288},{40,296},{48,304},{56,3... | collective-permute-start | bytes 10616840 | tf_op jit(solution)/shard_map/ppermute | solution.py:13
  144.8 1.9 collective-permute-start.4
  146.7 0.1 mul.26
  146.8 0.1 mul.27
  146.9 150.5 %collective-permute-done.3 = bf16[1024,1728]{0,1:T(8,128)(2,1)} collective-permute-done((bf16[1024,1728]{0,1:T(8,128)(2,1)}, bf16[1024,1728]{0,1:T(8,128)(2,1)}, u32[]{:S(2)}, u32[]{:S(2)}) %collective-permute-start.3) | collective-permute-done | bytes 3538976 | tf_op jit(solution)/shard_map/ppermute | solution.py:13
  297.4 8.6 %fusion = f32[320,1728]{1,0:T(8,128)S(1)} fusion(bf16[1,2048,320]{1,2,0:T(8,128)(2,1)S(1)} %copy-done, bf16[1024,1728]{0,1:T(8,128)(2,1)} %maximum_select_fusion.1, bf16[1024,1728]{0,1:T(8,128)(2,1)} %collective-permute-done.3, pred[]{:T(512)S(6)} %eq.36, bf16[1,320,1728]{2,1,0:T(8,128)(2,1)} %param.8), kind=kOutput, calls=%fused_computation.3 | convolution fusion | flops 2297880576 | bytes 11706369 | tf_op jit(solution)/shard_map/dot_general | solution.py:42
  305.9 1.4 copy-done.1
  307.3 1.9 fusion.22
  309.2 0.1 mul.29
  309.3 0.2 mul.30
  309.5 0.9 broadcast_multiply_fusion
  310.4 0.0 all-reduce.3.cloned.1.call-update
  310.5 0.0 all-reduce.5.cloned.1.call-start
  310.6 0.0 collective-permute-done.4
  310.6 0.1 maximum_select_fusion.8
  310.7 3.4 collective-permute-start.5
  314.1 189.0 %all-reduce.3.cloned.1.call-done = f32[5120,32]{0,1:T(8,128)} async-done(((f32[5120,32]{0,1:T(8,128)}), f32[5120,32]{0,1:T(8,128)}) %all-reduce.3.cloned.1.call-update) | async-done | bytes 655376 | tf_op jit(solution)/shard_map/psum | solution.py:57
  503.1 2.0 fusion.23
  505.1 0.1 copy.10
  505.2 2.9 cholesky.16
  508.1 0.6 compare_reduce_fusion
  508.8 0.7 fusion.15
  509.4 2.4 custom-call.7
  511.8 1.1 fusion.13
  513.0 7.0 fusion.24
  520.0 0.0 all-reduce.5.cloned.1.call-update
  520.0 0.2 reduce-scatter.2.cloned.1.call-start
  520.2 0.0 collective-permute-done.5
  520.3 11.4 %fusion.2 = f32[2048,320]{0,1:T(8,128)} fusion(bf16[1024,1728]{0,1:T(8,128)(2,1)} %maximum_select_fusion.1, bf16[1024,1728]{0,1:T(8,128)(2,1)} %collective-permute-done.3, pred[]{:T(512)S(6)} %eq.36, bf16[160,1728]{1,0:T(8,128)(2,1)S(1)} %maximum_select_fusion.8, bf16[160,1728]{1,0:T(8,128)(2,1)S(1)} %collective-permute-done.5, pred[]{:T(512)S(6)} %eq.40), kind=kOutput, calls=%fused_computation.7 | convolution fusion | flops 2301751296 | bytes 10805250 | tf_op jit(solution)/shard_map/dot_general | solution.py:47
  531.6 0.0 reduce-scatter.2.cloned.1.call-update
  531.7 185.3 %all-reduce.5.cloned.1.call-done = f32[1728,32]{1,0:T(8,128)} async-done(((f32[1728,32]{1,0:T(8,128)}), f32[1728,32]{1,0:T(8,128)}) %all-reduce.5.cloned.1.call-update) | async-done | bytes 221200 | tf_op jit(solution)/shard_map/psum | solution.py:71
  717.0 3.4 fusion.10
  720.4 0.8 dynamic-slice_convert_fusion
  721.1 1.2 fusion.3
  722.4 1.7 convert_bitcast_fusion
  (12 shorter events, 0.1 us)
Async XLA Ops:
  8.0 289.4 %copy-start = (bf16[1,2048,320]{1,2,0:T(8,128)(2,1)S(1)}, bf16[1,2048,320]{1,2,0:T(8,128)(2,1)}, u32[]{:S(2)}) copy-start(bf16[1,2048,320]{1,2,0:T(8,128)(2,1)} %param.5) | copy-start | bytes 3932164
  8.0 495.1 %all-reduce.3.cloned.1.call-start = ((), (), s32[]{:S(2)}) async-start(), calls=%async_computation.2 | async-start | bytes 1310720 | tf_op jit(solution)/shard_map/psum | solution.py:57
  8.1 15.6 %collective-permute-start = (bf16[128,1728]{0,1:T(8,128)(2,1)}, bf16[128,1728]{0,1:T(8,128)(2,1)S(1)}, u32[]{:S(2)}, u32[]{:S(2)}) collective-permute-start(bf16[128,1728]{0,1:T(8,128)(2,1)} %bitcast.33), channel_id=1, source_target_pairs={{0,32},{8,40},{16,48},{24,56},{32,0},{40,8},{48,16},{56,24},{64,96... | collective-permute-start | bytes 1327112 | tf_op jit(solution)/shard_map/ppermute | solution.py:13
  25.1 4.3 copy-start.3
  25.2 23.2 %collective-permute-start.1 = (bf16[256,1728]{0,1:T(8,128)(2,1)S(1)}, bf16[256,1728]{0,1:T(8,128)(2,1)}, u32[]{:S(2)}, u32[]{:S(2)}) collective-permute-start(bf16[256,1728]{0,1:T(8,128)(2,1)S(1)} %maximum_select_fusion.7), channel_id=1, source_target_pairs={{0,64},{8,72},{16,80},{24,88},{32,96},{40,104},{48,112},{56,120},{... | collective-permute-start | bytes 2654216 | tf_op jit(solution)/shard_map/ppermute | solution.py:13
  50.8 81.2 %collective-permute-start.2 = (bf16[512,1728]{0,1:T(8,128)(2,1)S(1)}, bf16[512,1728]{0,1:T(8,128)(2,1)}, u32[]{:S(2)}, u32[]{:S(2)}) collective-permute-start(bf16[512,1728]{0,1:T(8,128)(2,1)S(1)} %maximum_select_fusion.2), channel_id=1, source_target_pairs={{0,128},{8,136},{16,144},{24,152},{32,160},{40,168},{48,176},{56,1... | collective-permute-start | bytes 5308424 | tf_op jit(solution)/shard_map/ppermute | solution.py:13
  56.9 87.9 %copy-start.4 = (bf16[80,1728]{1,0:T(8,128)(2,1)S(1)}, bf16[80,1728]{1,0:T(8,128)(2,1)}, u32[]{:S(2)}) copy-start(bf16[80,1728]{1,0:T(8,128)(2,1)} %param.7) | copy-start | bytes 829444
  136.3 161.0 %collective-permute-start.3 = (bf16[1024,1728]{0,1:T(8,128)(2,1)}, bf16[1024,1728]{0,1:T(8,128)(2,1)}, u32[]{:S(2)}, u32[]{:S(2)}) collective-permute-start(bf16[1024,1728]{0,1:T(8,128)(2,1)} %maximum_select_fusion.1), channel_id=1, source_target_pairs={{0,256},{8,264},{16,272},{24,280},{32,288},{40,296},{48,304},{56,3... | collective-permute-start | bytes 10616840 | tf_op jit(solution)/shard_map/ppermute | solution.py:13
  144.8 165.8 %collective-permute-start.4 = (bf16[80,1728]{1,0:T(8,128)(2,1)S(1)}, bf16[80,1728]{1,0:T(8,128)(2,1)S(1)}, u32[]{:S(2)}, u32[]{:S(2)}) collective-permute-start(bf16[80,1728]{1,0:T(8,128)(2,1)S(1)} %copy-done.4), channel_id=1, source_target_pairs={{0,8},{8,0},{16,24},{24,16},{32,40},{40,32},{48,56},{56,48},{64,72... | collective-permute-start | bytes 829448 | tf_op jit(solution)/shard_map/ppermute | solution.py:13
  146.9 160.4 %copy-start.5 = (f32[1728,32]{0,1:T(8,128)S(1)}, f32[1728,32]{0,1:T(8,128)}, u32[]{:S(2)}) copy-start(f32[1728,32]{0,1:T(8,128)} %param.9) | copy-start | bytes 663556
  305.9 1.4 copy-start.1
  310.5 406.5 %all-reduce.5.cloned.1.call-start = ((), (), s32[]{:S(2)}) async-start(), calls=%async_computation.3 | async-start | bytes 1769472 | tf_op jit(solution)/shard_map/psum | solution.py:71
  310.7 209.6 %collective-permute-start.5 = (bf16[160,1728]{1,0:T(8,128)(2,1)S(1)}, bf16[160,1728]{1,0:T(8,128)(2,1)S(1)}, u32[]{:S(2)}, u32[]{:S(2)}) collective-permute-start(bf16[160,1728]{1,0:T(8,128)(2,1)S(1)} %maximum_select_fusion.8), channel_id=1, source_target_pairs={{0,16},{8,24},{16,0},{24,8},{32,48},{40,56},{48,32},{56,40},{64,80... | collective-permute-start | bytes 1658888 | tf_op jit(solution)/shard_map/ppermute | solution.py:13
  520.0 202.3 %reduce-scatter.2.cloned.1.call-start = ((), (), s32[]{:S(2)}) async-start(), calls=%async_computation.1 | async-start | bytes 2949120 | tf_op jit(solution)/shard_map/reduce_scatter | solution.py:46
  717.0 4.1 copy-start.2
Sparse Core Ops, SparseCore 0:
  310.6 192.4 all-reduce.2
  520.1 196.8 all-reduce.4
Sparse Core Ops, SparseCore 1:
  531.8 42.0 reduce-scatter.1
where the time goes:
time: 732 us; the launch traced here: 731 us
  waiting for transfers between devices  629 us (86%)
  matrix products  35.3 us (5%)
  starting transfers between devices  29.5 us (4%)
  other arithmetic  18.8 us (3%)
  between operations  15.9 us (2%)
    ppermute x6, waiting for transfers between devices, partner_2(): lax.ppermute(value, axis, [(i, i ^ 1 << stride) for i in range(lax.axis_s...  255 us
    psum x1, waiting for transfers between devices, body(): whole_factor = lax.psum(padded, 'dp')  189 us
    psum x1, waiting for transfers between devices, body(): second_factor = lax.psum(local_second, 'dp') / replicas  185 us
    ppermute x6, starting transfers between devices, partner_2(): lax.ppermute(value, axis, [(i, i ^ 1 << stride) for i in range(lax.axis_s...  29.2 us
  transfers between devices with their start and end apart: 9, of which 6 were waited for; matrix products, arithmetic and copies ran while one was open for 6% of the time, Pallas kernels for 0%

commit v1 on v0

v1 whole, which is shorter than its diff:
```python
import jax
import jax.numpy as jnp
from jax import lax
from jax.experimental import pallas as pl
from jax.experimental.pallas import tpu as pltpu
from jax.sharding import PartitionSpec as P

F32 = jnp.float32
BF16 = jnp.bfloat16
MESH = pl.DeviceIdType.MESH
NZ = 8
NO = 8
NY = 8
TOK = 128
HIDDEN = 1728
WIDTH = 320
RANK = 32
ROWS = 80
NN = (((1,), (0,)), ((), ()))
NT = (((1,), (1,)), ((), ()))
TN = (((0,), (0,)), ((), ()))


def dot(a, b, dims):
    return lax.dot_general(a, b, dims, preferred_element_type=F32)


def split3(value):
    high = value.astype(BF16)
    rest = value - high.astype(F32)
    middle = rest.astype(BF16)
    low = (rest - middle.astype(F32)).astype(BF16)
    return high, middle, low


def dot_rows(value, exact, dims):
    rows = value.shape[0]
    out = dot(jnp.concatenate(split3(value), axis=0), exact, dims)
    return out[:rows] + out[rows : 2 * rows] + out[2 * rows :]


def dot_full(a, b, dims):
    return lax.dot_general(a, b, dims, precision=lax.Precision.HIGHEST, preferred_element_type=F32)


def kernel(
    x_hbm, g_hbm, w_hbm, e_hbm, f_hbm,
    dx_out, err_out, upd_out,
    gbuf, xv, wslab, ev, fv, macc, abuf,
    part, rx, rxb,
    tbuf, pbuf, ybuf, yin, gram_own, gram_in, ymsg, yall,
    sbuf, sin, s2, s2in, s3, s4, gfull,
    lsem, gx_s, gx_r, gz_s, gz_r, w_s, w_r, t_s, t_r, tx_s, tx_r, p_s, p_r,
    yx_s, yx_r, yz_s, yz_r, s1_s, s1_r, s2_s, s2_r, s3_s, s3_r, s4_s, s4_r,
    dx_s, dx_r, dxb_r,
):
    me = lax.axis_index("dp")
    y = lax.axis_index("tensor")
    z = me // NO
    slot = me % NO
    rep = me % 4
    xh = slot // 4
    own = 2 * z + xh

    def at_z(j):
        return {"dp": ((z + j + NZ) % NZ) * NO + slot, "tensor": y}

    def at_slot(j):
        return {"dp": me - slot + (slot + j) % NO, "tensor": y}

    def at_rep(j):
        return {"dp": me - rep + (rep + j) % 4, "tensor": y}

    partner = {"dp": me + 4 - 8 * xh, "tensor": y}

    def at_y(j):
        return {"dp": me, "tensor": (y + j + NY) % NY}

    def remote(src, dst, send, recv, device):
        return pltpu.make_async_remote_copy(
            src_ref=src, dst_ref=dst, send_sem=send, recv_sem=recv,
            device_id=device, device_id_type=MESH,
        )

    sent = []

    def send(*args):
        copy = remote(*args)
        copy.start()
        sent.append(copy)
        return copy

    my_rows = pl.ds(pl.multiple_of(rep * ROWS, 16), ROWS)
    local = [
        pltpu.make_async_copy(g_hbm.at[0], gbuf.at[own], lsem.at[0]),
        pltpu.make_async_copy(f_hbm, fv, lsem.at[1]),
        pltpu.make_async_copy(e_hbm.at[0], ev, lsem.at[2]),
        pltpu.make_async_copy(x_hbm.at[0], xv, lsem.at[3]),
        pltpu.make_async_copy(w_hbm, wslab.at[my_rows], lsem.at[4]),
    ]
    for copy in local:
        copy.start()

    barrier = pltpu.get_barrier_semaphore()
    greet = [at_z(j) for j in range(1, NZ)] + [at_slot(j) for j in range(1, NO)] + [at_y(1), at_y(-1)]
    for device in greet:
        pl.semaphore_signal(barrier, inc=1, device_id=device, device_id_type=MESH)
    pl.semaphore_wait(barrier, len(greet))

    def chunk_of(shift, other):
        return 2 * ((z + shift + NZ) % NZ) + (1 - xh if other else xh)

    def ring(direction, hop, other):
        sign = 1 if direction == 0 else -1
        chunk = chunk_of(-sign * (hop - 1), other)
        k = direction * 8 + (hop - 1) * 2 + other
        return remote(gbuf.at[chunk], gbuf.at[chunk], gz_s.at[k], gz_r.at[k], at_z(sign))

    def ring_send(direction, hop, other):
        copy = ring(direction, hop, other)
        copy.start()
        sent.append(copy)

    def ring_wait(direction, hop, other):
        ring(direction, hop, other).wait_recv()

    local[0].wait()
    ring_send(0, 1, 0)
    ring_send(1, 1, 0)
    swap = send(gbuf.at[own], gbuf.at[own], gx_s.at[0], gx_r.at[0], partner)

    local[1].wait()
    factor = fv[...].T
    factor3 = jnp.concatenate(split3(factor), axis=0)

    def add3(v):
        return v[:RANK] + v[RANK : 2 * RANK] + v[2 * RANK :]

    tbuf[z, xh] = add3(dot(factor3, gbuf[own], NT))
    tz = [send(tbuf.at[z, xh], tbuf.at[z, xh], t_s.at[j - 1], t_r.at[j - 1], at_z(j)) for j in range(1, NZ)]
    local[4].wait()
    wcopies = [
        send(wslab.at[my_rows], wslab.at[my_rows], w_s.at[j - 1], w_r.at[j - 1], at_rep(j)) for j in range(1, 4)
    ]
    local[2].wait()
    local[3].wait()
    macc[...] = ev[...].astype(F32)
    p_part = add3(dot(factor3, ev[...], NT))

    pending = []

    def dx_hop(chunk, stage):
        root = chunk // 2
        d = (root - y + NY) % NY
        up = remote(part.at[chunk], rx.at[chunk], dx_s.at[chunk], dx_r.at[chunk], at_y(1))
        down = remote(part.at[chunk], rx.at[chunk], dx_s.at[chunk], dx_r.at[chunk], at_y(-1))
        down_root = remote(part.at[chunk], rxb.at[chunk % 2], dx_s.at[chunk], dxb_r.at[chunk % 2], at_y(-1))
        if stage == 0:

            @pl.when(d == 4)
            def _():
                up.start()

            @pl.when(d == 5)
            def _():
                down.start()

        elif stage < 4:
            up_d = 4 - stage
            down_d = 5 + stage

            @pl.when(d == up_d)
            def _():
                up.wait_recv()
                part[chunk] += rx[chunk]
                up.start()

            if down_d < NY:

                @pl.when(d == down_d)
                def _():
                    down.wait_recv()
                    part[chunk] += rx[chunk]
                    if down_d == NY - 1:
                        down_root.start()
                    else:
                        down.start()

        else:

            @pl.when(d == 0)
            def _():
                up.wait_recv()
                down_root.wait_recv()
                total = part[chunk] + rx[chunk] + rxb[chunk % 2]
                row = pl.multiple_of((chunk % 2) * TOK, TOK)
                dx_out[0, pl.ds(row, TOK), :] = total.astype(BF16)

    def advance():
        for entry in pending:
            if entry[1] <= 4:
                dx_hop(entry[0], entry[1])
                entry[1] += 1

    def accumulate(chunk):
        tokens = xv[pl.ds(pl.multiple_of(chunk * TOK, TOK), TOK), :]
        for start in range(0, HIDDEN, 512):
            stop = min(start + 512, HIDDEN)
            macc[:, start:stop] += dot(tokens, gbuf[chunk, :, start:stop], TN)

    def input_part(chunk):
        part[chunk] = dot(gbuf[chunk], wslab[...], NT)
        dx_hop(chunk, 0)
        pending.append([chunk, 1])

    def process(chunk):
        accumulate(chunk)
        input_part(chunk)

    accumulate(own)

    for copy in tz:
        copy.wait_recv()
    tx = send(tbuf.at[:, xh], tbuf.at[:, xh], tx_s.at[0], tx_r.at[0], partner)
    tx.wait_recv()
    t_all = jnp.concatenate([tbuf[i // 2, i % 2] for i in range(2 * NZ)], axis=1)
    pbuf[rep] = p_part + dot_rows(t_all, xv[...], NN)
    pcopies = [send(pbuf.at[rep], pbuf.at[rep], p_s.at[j - 1], p_r.at[j - 1], at_rep(j)) for j in range(1, 4)]

    swap.wait_recv()
    ring_send(0, 1, 1)
    ring_send(1, 1, 1)
    for copy in wcopies:
        copy.wait_recv()
    input_part(own)
    process(chunk_of(0, 1))

    for copy in pcopies:
        copy.wait_recv()
    p_t = pbuf[0] + pbuf[1] + pbuf[2] + pbuf[3]
    gram = dot_full(p_t, p_t, NT)
    for i in range(4):
        gram_own[:, RANK * i : RANK * (i + 1)] = gram[8 * i : 8 * (i + 1), :]
    y_t = dot_rows(p_t, xv[...], NT)
    for i in range(2 * NZ):
        ybuf[i % 2, i // 2] = y_t[:, TOK * i : TOK * (i + 1)]
    yx = [
        send(ybuf.at[1 - xh], yin, yx_s.at[0], yx_r.at[0], partner),
        send(gram_own, gram_in, yx_s.at[1], yx_r.at[1], partner),
    ]

    def ring_group(hop, other):
        last = NZ // 2
        new = []
        for direction in range(2):
            if hop == last and direction != other:
                continue
            ring_wait(direction, hop, other)
            if hop + 1 < last or (hop + 1 == last and direction == other):
                ring_send(direction, hop + 1, other)
            new.append(chunk_of(-hop if direction == 0 else hop, other))
        advance()
        for chunk in new:
            process(chunk)

    ring_group(1, 0)

    for copy in yx:
        copy.wait_recv()
    pair_gram = gram_own[...] + gram_in[...]
    for i in range(NZ):
        ymsg[i, :RANK] = ybuf[xh, i] + yin[i]
        ymsg[i, RANK:] = pair_gram
    yall[z] = ymsg[z]
    yz = [
        send(ymsg.at[(z + j) % NZ], yall.at[z], yz_s.at[j - 1], yz_r.at[j - 1], at_z(j)) for j in range(1, NZ)
    ]

    ring_group(1, 1)

    for copy in yz:
        copy.wait_recv()
    y_sum = yall[0]
    for i in range(1, NZ):
        y_sum = y_sum + yall[i]
    s_t = dot_rows(p_t, ev[...], NN) + dot_rows(y_sum[:RANK], gbuf[own], NN)
    sbuf[6] = jnp.zeros_like(sbuf[6])
    sbuf[7] = jnp.zeros_like(sbuf[7])
    for i in range(7):
        width = min(256, HIDDEN - 256 * i)
        sbuf[i, :, :width] = s_t[:, 256 * i : 256 * i + width]
    sin[slot] = sbuf[slot]
    s1 = [
        send(sbuf.at[(slot + j) % NO], sin.at[slot], s1_s.at[j - 1], s1_r.at[j - 1], at_slot(j))
        for j in range(1, NO)
    ]

    for i in range(4):
        gfull[8 * i : 8 * (i + 1), :RANK] = y_sum[RANK:, RANK * i : RANK * (i + 1)]
    row_id = lax.broadcasted_iota(jnp.int32, (RANK, 128), 0)
    lane_id = lax.broadcasted_iota(jnp.int32, (RANK, 128), 1)
    work = jnp.where(lane_id < RANK, gfull[...], jnp.where(lane_id == row_id + RANK, 1.0, 0.0))
    for j in range(RANK):
        ratio = work[:, j : j + 1] / work[j : j + 1, j : j + 1]
        ratio = jnp.where(row_id[:, :1] > j, ratio, 0.0)
        work = work - ratio * work[j : j + 1, :]
    pivots = jnp.sum(jnp.where(lane_id == row_id, work, 0.0), axis=1, keepdims=True)
    inverse = (work / jnp.sqrt(pivots))[:, RANK : 2 * RANK]
    basis = dot_full(inverse, p_t, NN)

    ring_group(2, 0)

    for copy in s1:
        copy.wait_recv()
    total = sin[0]
    for i in range(1, NO):
        total = total + sin[i]
    for i in range(NZ):
        s2[i] = total[8 * (i // 2) : 8 * (i // 2) + 8, 128 * (i % 2) : 128 * (i % 2) + 128]
    s2in[z] = s2[z]
    s2c = [
        send(s2.at[(z + j) % NZ], s2in.at[z], s2_s.at[j - 1], s2_r.at[j - 1], at_z(j)) for j in range(1, NZ)
    ]

    ring_group(2, 1)

    for copy in s2c:
        copy.wait_recv()
    tile = s2in[0]
    for i in range(1, NZ):
        tile = tile + s2in[i]
    s3[z] = tile
    s3c = [send(s3.at[z], s3.at[z], s3_s.at[j - 1], s3_r.at[j - 1], at_z(j)) for j in range(1, NZ)]

    ring_group(3, 0)

    for copy in s3c:
        copy.wait_recv()
    for i in range(NZ):
        s4[slot, 8 * (i // 2) : 8 * (i // 2) + 8, 128 * (i % 2) : 128 * (i % 2) + 128] = s3[i]
    s4c = [
        send(s4.at[slot], s4.at[slot], s4_s.at[j - 1], s4_r.at[j - 1], at_slot(j)) for j in range(1, NO)
    ]

    ring_group(3, 1)

    for copy in s4c:
        copy.wait_recv()
    s_all = jnp.concatenate([s4[i] for i in range(7)], axis=1)[:, :HIDDEN]
    second = dot_full(inverse, s_all, NN) * 0.25
    bh, bm, bl = split3(basis)
    qh, qm, ql = split3(second)
    left = jnp.concatenate([bh, bh, bm, bh, bl, bm], axis=0)
    right = jnp.concatenate([qh, qm, qh, ql, qh, qm], axis=0)
    for start in range(0, HIDDEN, 512):
        stop = min(start + 512, HIDDEN)
        block = dot(left, right[:, start:stop], TN)
        abuf[:, start:stop] = block
        macc[:, start:stop] -= block
    upd_out[...] = abuf[my_rows, :].astype(BF16)

    ring_group(4, 0)
    ring_group(4, 1)
    err_out[0] = macc[...].astype(BF16)
    for _ in range(4):
        advance()

    for copy in sent:
        copy.wait_send()
    for shift in range(NZ):
        for other in range(2):
            chunk = chunk_of(shift, other)

            @pl.when((chunk // 2 - y + NY) % NY != 0)
            def _():
                remote(
                    part.at[chunk], rx.at[chunk], dx_s.at[chunk], dx_r.at[chunk], at_y(1)
                ).wait_send()


def body(activations, cotangent, weight, error_buffer, warm_factor):
    dma = pltpu.SemaphoreType.DMA
    sems = [
        dma((5,)), dma((1,)), dma((1,)), dma((16,)), dma((16,)), dma((3,)), dma((3,)), dma((7,)), dma((7,)),
        dma((1,)), dma((1,)), dma((3,)), dma((3,)), dma((2,)), dma((2,)), dma((7,)), dma((7,)),
        dma((7,)), dma((7,)), dma((7,)), dma((7,)), dma((7,)), dma((7,)), dma((7,)), dma((7,)),
        dma((16,)), dma((16,)), dma((2,)),
    ]
    vmem = pltpu.VMEM
    scratch = [
        vmem((16, TOK, HIDDEN), BF16),
        vmem((16 * TOK, WIDTH), BF16),
        vmem((WIDTH, HIDDEN), BF16),
        vmem((WIDTH, HIDDEN), BF16),
        vmem((HIDDEN, RANK), F32),
        vmem((WIDTH, HIDDEN), F32),
        vmem((WIDTH, HIDDEN), F32),
        vmem((16, TOK, WIDTH), F32),
        vmem((16, TOK, WIDTH), F32),
        vmem((2, TOK, WIDTH), F32),
        vmem((NZ, 2, RANK, TOK), F32),
        vmem((4, RANK, WIDTH), F32),
        vmem((2, NZ, RANK, TOK), F32),
        vmem((NZ, RANK, TOK), F32),
        vmem((8, 128), F32),
        vmem((8, 128), F32),
        vmem((NZ, RANK + 8, 128), F32),
        vmem((NZ, RANK + 8, 128), F32),
        vmem((NO, RANK, 256), F32),
        vmem((NO, RANK, 256), F32),
        vmem((NZ, 8, 128), F32),
        vmem((NZ, 8, 128), F32),
        vmem((NZ, 8, 128), F32),
        vmem((NO, RANK, 256), F32),
        vmem((RANK, 128), F32),
    ]
    anyspec = pl.BlockSpec(memory_space=pl.ANY)
    vspec = pl.BlockSpec(memory_space=pltpu.VMEM)
    return pl.pallas_call(
        kernel,
        out_shape=(
            jax.ShapeDtypeStruct((1, 2 * TOK, WIDTH), BF16),
            jax.ShapeDtypeStruct((1, WIDTH, HIDDEN), BF16),
            jax.ShapeDtypeStruct((ROWS, HIDDEN), BF16),
        ),
        in_specs=[anyspec] * 5,
        out_specs=(vspec, vspec, vspec),
        scratch_shapes=scratch + sems,
        compiler_params=pltpu.CompilerParams(
            collective_id=0, has_side_effects=True, vmem_limit_bytes=56 * 1024 * 1024
        ),
        cost_estimate=pl.CostEstimate(flops=4600000000, bytes_accessed=8000000, transcendentals=0),
    )(activations, cotangent, weight, error_buffer, warm_factor)


def solution(mesh):
    in_specs = (
        P("dp", None, None),
        P("dp", None, "tensor"),
        P("dp", "tensor"),
        P("dp", None, "tensor"),
        P("tensor", None),
    )
    out_specs = (P("dp", "tensor", None), P("dp", None, "tensor"), P("dp", "tensor"))
    return jax.shard_map(body, mesh=mesh, in_specs=in_specs, out_specs=out_specs, check_vma=False)
```

time: 732 us -> 152 us (0.21)
  the two profiles are of different devices: /device:TPU:40 before, /device:TPU:32 now
where the time goes in v1:
time: 152 us
  Pallas kernels  140 us (92%)
  local copies, waits for them, and re-layouts  10.6 us (7%)
    pallas_call x1, Pallas kernels, body(): pl.pallas_call(kernel, out_shape=(jax.ShapeDtypeStruct((1, 2 * TOK, WIDTH...  140 us
    unnamed x9, local copies, waits for them, and re-layouts  8.93 us

profile of v1, /device:TPU:32, one launch (start us, length us, event | category | flops | bytes accessed | tf_op | source)
XLA Modules:
  0.0 151.6 jit_solution(4656306803538505782)
XLA Ops:
  0.6 0.0 copy-start
  0.6 2.1 %copy.9.g_hbm = bf16[1,128,1728]{2,1,0:T(8,128)(2,1)} copy(bf16[1,128,1728]{1,2,0:T(8,128)(2,1)} %param.6) | data formatting | bytes 884736 | tf_op args[1]
  2.7 2.2 %copy.10.f_hbm = f32[1728,32]{1,0:T(8,128)} copy(f32[1728,32]{0,1:T(8,128)} %param.9) | data formatting | bytes 442368 | tf_op args[4]
  4.9 0.0 copy-done
  4.9 1.6 %copy.8.x_hbm = bf16[1,2048,320]{2,1,0:T(8,128)(2,1)} copy(bf16[1,2048,320]{1,2,0:T(8,128)(2,1)S(1)} %copy-done) | data formatting | bytes 2621440 | tf_op args[0]
  6.5 140.3 %shard_map.76 = (bf16[1,256,320]{2,1,0:T(8,128)(2,1)}, bf16[1,320,1728]{2,1,0:T(8,128)(2,1)}, bf16[80,1728]{1,0:T(8,128)(2,1)}) custom-call(bf16[1,2048,320]{2,1,0:T(8,128)(2,1)} %copy.8.x_hbm, bf16[1,128,1728]{2,1,0:T(8,128)(2,1)} %copy.9.g_hbm, bf16[80,1728]{1,0:T(8,128)(2,1)} %w_hbm.1, bf16[1,320,1728]{2,1,0:T(8,128)(2,1)} %e_hbm.1, f32[1728,32]{1,0:T(8,128)} %copy.10.f_hbm), custom_call_target="tpu_custom_call" | custom-call | flops 4600000000 | bytes 8000000 | tf_op jit(solution)/shard_map/pallas_call | solution.py:419
  146.8 1.7 %copy.11 = bf16[1,256,320]{1,2,0:T(8,128)(2,1)} copy(bf16[1,256,320]{2,1,0:T(8,128)(2,1)} %get-tuple-element.3) | data formatting | bytes 327680 | tf_op jit(solution)/shard_map/pallas_call | solution.py:419
  148.5 0.0 copy-start.1
  148.5 2.4 %copy.14 = bf16[1,320,1728]{2,1,0:T(8,128)(2,1)} copy(bf16[1,320,1728]{2,1,0:T(8,128)(2,1)} %get-tuple-element.10) | data formatting | bytes 2211840
  150.9 0.0 copy-done.1
  150.9 0.7 copy.15
Async XLA Ops:
  0.6 4.3 %copy-start = (bf16[1,2048,320]{1,2,0:T(8,128)(2,1)S(1)}, bf16[1,2048,320]{1,2,0:T(8,128)(2,1)}, u32[]{:S(2)}) copy-start(bf16[1,2048,320]{1,2,0:T(8,128)(2,1)} %param.5) | copy-start | bytes 3932164
  148.5 2.4 %copy-start.1 = (bf16[80,1728]{1,0:T(8,128)(2,1)S(1)}, bf16[80,1728]{1,0:T(8,128)(2,1)}, u32[]{:S(2)}) copy-start(bf16[80,1728]{1,0:T(8,128)(2,1)} %get-tuple-element.11) | copy-start | bytes 829444

commit v2 on v0

v2 whole, which is shorter than its diff:
```python
import jax
import jax.numpy as jnp
from jax import lax
from jax.experimental import pallas as pl
from jax.experimental.pallas import tpu as pltpu
from jax.sharding import PartitionSpec as P

F32 = jnp.float32
BF16 = jnp.bfloat16
MESH = pl.DeviceIdType.MESH
NZ = 8
NO = 8
NY = 8
TOK = 128
HIDDEN = 1728
WIDTH = 320
RANK = 32
ROWS = 80
PIECES = 6
PIECE = HIDDEN // PIECES
SUBS = 4
SPACING = 8
DEPTH = 4
SUB = WIDTH // SUBS
NN = (((1,), (0,)), ((), ()))
NT = (((1,), (1,)), ((), ()))
TN = (((0,), (0,)), ((), ()))


def dot(a, b, dims):
    return lax.dot_general(a, b, dims, preferred_element_type=F32)


def split3(value):
    high = value.astype(BF16)
    rest = value - high.astype(F32)
    middle = rest.astype(BF16)
    low = (rest - middle.astype(F32)).astype(BF16)
    return high, middle, low


def dot_rows(value, exact, dims):
    rows = value.shape[0]
    out = dot(jnp.concatenate(split3(value), axis=0), exact, dims)
    return out[:rows] + out[rows : 2 * rows] + out[2 * rows :]


def dot_full(a, b, dims):
    return lax.dot_general(a, b, dims, precision=lax.Precision.HIGHEST, preferred_element_type=F32)


def kernel(
    x_hbm, g_hbm, w_hbm, e_hbm, f_hbm,
    dx_out, err_out, upd_out,
    gbuf, xv, wslab, ev, fv, macc, abuf,
    part, rx, rxb, p_part,
    tbuf, pbuf, gram_own, ymsg, yall,
    sbuf, sin, s2, s2in, s3, s4, gfull,
    lsem, gx_s, gx_r, gz_s, gz_r, w_s, w_r, t_s, t_r, p_s, p_r,
    yz_s, yz_r, s1_s, s1_r, s2_s, s2_r, s3_s, s3_r, s4_s, s4_r,
    dx_s, dx_r, dxb_r,
):
    me = lax.axis_index("dp")
    y = lax.axis_index("tensor")
    z = me // NO
    slot = me % NO
    rep = me % 4
    xh = slot // 4
    own = 2 * z + xh

    def at_z(j):
        return {"dp": ((z + j + NZ) % NZ) * NO + slot, "tensor": y}

    def at_slot(j):
        return {"dp": me - slot + (slot + j) % NO, "tensor": y}

    def at_rep(j):
        return {"dp": me - rep + (rep + j) % 4, "tensor": y}

    partner = {"dp": me + 4 - 8 * xh, "tensor": y}

    def at_y(j):
        return {"dp": me, "tensor": (y + j + NY) % NY}

    def at_chunk(chunk):
        return {"dp": (chunk // 2) * NO + slot % 4 + 4 * (chunk % 2), "tensor": y}

    def remote(src, dst, send, recv, device):
        return pltpu.make_async_remote_copy(
            src_ref=src, dst_ref=dst, send_sem=send, recv_sem=recv,
            device_id=device, device_id_type=MESH,
        )

    sent = []

    def chain_send(*args):
        return send(*args)

    def send(*args):
        copy = remote(*args)
        copy.start()
        sent.append(copy)
        return copy

    my_rows = pl.ds(pl.multiple_of(rep * ROWS, 16), ROWS)
    local = [
        pltpu.make_async_copy(g_hbm.at[0], gbuf.at[own], lsem.at[0]),
        pltpu.make_async_copy(f_hbm, fv, lsem.at[1]),
        pltpu.make_async_copy(e_hbm.at[0], ev, lsem.at[2]),
        pltpu.make_async_copy(x_hbm.at[0], xv, lsem.at[3]),
        pltpu.make_async_copy(w_hbm, wslab.at[my_rows], lsem.at[4]),
    ]
    for copy in local:
        copy.start()

    barrier = pltpu.get_barrier_semaphore()
    greet = [at_chunk((own + j) % 16) for j in range(1, 16)] + [at_slot(j) for j in range(1, NO) if j != 4]
    greet += [at_y(j) for j in (-3, -2, -1, 1, 2, 3)]
    for device in greet:
        pl.semaphore_signal(barrier, inc=1, device_id=device, device_id_type=MESH)
    pl.semaphore_wait(barrier, len(greet))

    def chunk_of(shift, other):
        return 2 * ((z + shift + NZ) % NZ) + (1 - xh if other else xh)

    def pieces_of(direction, hop, other):
        if hop < NZ // 2:
            return range(PIECES)
        half = PIECES // 2
        return range(half) if direction == 0 else range(half, PIECES)

    def ring(direction, hop, other, piece):
        sign = 1 if direction == 0 else -1
        ref = gbuf.at[chunk_of(-sign * (hop - 1), other), pl.ds(piece * PIECE, PIECE)]
        k = ((direction * 4 + hop - 1) * 2 + other) * PIECES + piece
        return remote(ref, ref, gz_s.at[k], gz_r.at[k], at_z(sign))

    queues = [[], []]
    counts = [[0, 0], [0, 0]]

    def issue(direction):
        count = counts[direction]
        while queues[direction] and count[0] < count[1] + DEPTH:
            copy = ring(direction, *queues[direction].pop(0))
            copy.start()
            sent.append(copy)
            count[0] += 1

    def ring_send(direction, hop, other, piece):
        queues[direction].append((hop, other, piece))

    SHIFTS = (0, -3, 3, 4)

    def cross(k, piece):
        ref = gbuf.at[chunk_of(SHIFTS[k], 0), pl.ds(piece * PIECE, PIECE)]
        return remote(ref, ref, gx_s.at[k * PIECES + piece], gx_r.at[k * PIECES + piece], partner)

    def cross_send(k, piece):
        copy = cross(k, piece)
        copy.start()
        sent.append(copy)

    def cross_wait(k):
        for piece in range(PIECES):
            cross(k, piece).wait_recv()

    def arrive(hop, other, work):
        for step in range(len(pieces_of(0, hop, other))):
            for direction in range(2):
                piece = pieces_of(direction, hop, other)[step]
                ring(direction, hop, other, piece).wait_recv()
                counts[direction][1] += 1
                reach = 2 if other else 4
                if hop < reach and piece in pieces_of(direction, hop + 1, other):
                    ring_send(direction, hop + 1, other, piece)
                issue(direction)
                if not other and hop == 3:
                    cross_send(1 + direction, piece)
                if not other and hop == 4:
                    cross_send(3, piece)
            advance()
            for task in work.get(step, ()):
                task()

    local[0].wait()
    local[1].wait()

    factor3 = jnp.concatenate(split3(fv[...]), axis=0)

    def add3(v):
        return v[:RANK] + v[RANK : 2 * RANK] + v[2 * RANK :]

    tbuf[own] = add3(dot(factor3, gbuf[own], NN))
    tz = [
        chain_send(tbuf.at[own], tbuf.at[own], t_s.at[j - 1], t_r.at[j - 1], at_chunk((own + j) % 16))
        for j in range(1, 16)
    ]
    for piece in range(PIECES):
        ring_send(0, 1, 0, piece)
        ring_send(1, 1, 0, piece)
    issue(0)
    issue(1)
    local[4].wait()
    wcopies = [
        send(wslab.at[my_rows], wslab.at[my_rows], w_s.at[j - 1], w_r.at[j - 1], at_rep(j)) for j in range(1, 4)
    ]
    for piece in range(PIECES):
        cross_send(0, piece)
    local[2].wait()
    local[3].wait()
    macc[...] = ev[...].astype(F32)
    p_part[...] = add3(dot(factor3, ev[...], NT))

    pending = []

    def dx_hop(chunk, stage):
        turn = 1 - 2 * (chunk % 2)
        root = chunk // 2
        d = (turn * (root - y) + 2 * NY) % NY

        def near(sub, step):
            rows = pl.ds(sub * SUB, SUB)
            return remote(
                part.at[chunk, rows], rx.at[chunk, rows], dx_s.at[chunk], dx_r.at[chunk * SUBS + sub], at_y(step)
            )

        def last(sub, distance):
            rows = pl.ds(sub * SUB, SUB)
            k = chunk % 2 * NY + distance
            return remote(
                part.at[chunk, rows], rxb.at[k, rows], dx_s.at[chunk], dxb_r.at[k * SUBS + sub],
                {"dp": me, "tensor": root},
            )

        if stage == 0:

            @pl.when((d == 4) | (d == 2))
            def _():
                for sub in range(SUBS):
                    near(sub, turn).start()

            @pl.when(d == 5)
            def _():
                for sub in range(SUBS):
                    near(sub, -turn).start()

            @pl.when(d == 7)
            def _():
                for sub in range(SUBS):
                    last(sub, d).start()

        elif stage == 1:

            @pl.when((d == 1) | (d == 3) | (d == 6))
            def _():
                for sub in range(SUBS):
                    near(sub, turn).wait_recv()
                    rows = pl.ds(sub * SUB, SUB)
                    part[chunk, rows] += rx[chunk, rows]
                    last(sub, d).start()

        else:

            @pl.when(d == 0)
            def _():
                lane = pl.multiple_of((chunk % 2) * TOK, TOK)
                for sub in range(SUBS):
                    rows = pl.ds(sub * SUB, SUB)
                    total = part[chunk, rows]
                    for distance in (7, 1, 6, 3):
                        arrived = remote(
                            part.at[chunk, rows], rxb.at[chunk % 2 * NY + distance, rows], dx_s.at[chunk],
                            dxb_r.at[(chunk % 2 * NY + distance) * SUBS + sub], at_y(1),
                        )
                        arrived.wait_recv()
                        total += rxb[chunk % 2 * NY + distance, rows]
                    dx_out[0, rows, pl.ds(lane, TOK)] = total.astype(BF16)

    clock = [0]

    def advance(spacing=SPACING):
        clock[0] += 1
        for stage in (1,):
            for entry in pending:
                if entry[1] == stage and clock[0] - entry[2] >= spacing:
                    dx_hop(entry[0], stage)
                    entry[1:] = [stage + 1, clock[0]]

    def accumulate(chunk):
        tokens = xv[:, pl.ds(pl.multiple_of(chunk * TOK, TOK), TOK)]
        for start in range(0, HIDDEN, 512):
            stop = min(start + 512, HIDDEN)
            macc[:, start:stop] += dot(tokens, gbuf[chunk, start:stop, :], NT)

    def process(*chunks):
        for chunk in chunks:
            accumulate(chunk)
        for chunk in chunks:
            part[chunk] = dot(wslab[...], gbuf[chunk], NN)
            dx_hop(chunk, 0)
            pending.append([chunk, 1, clock[0]])

    flight = {}

    def wait_for(name):
        for copy in flight[name]:
            copy.wait_recv()

    def left_factor():
        wait_for("tz")
        t_all = jnp.concatenate([tbuf[i] for i in range(16)], axis=1)
        pbuf[rep] = p_part[...] + dot_rows(t_all, xv[...], NT)
        flight["p"] = [
            chain_send(pbuf.at[rep], pbuf.at[rep], p_s.at[j - 1], p_r.at[j - 1], at_rep(j)) for j in range(1, 4)
        ]

    def project_tokens():
        wait_for("p")
        p_t = pbuf[0] + pbuf[1] + pbuf[2] + pbuf[3]
        p_part[...] = p_t
        gram = dot_full(p_t, p_t, NT)
        for i in range(4):
            gram_own[:, RANK * i : RANK * (i + 1)] = gram[8 * i : 8 * (i + 1), :]
        packed = gram_own[...]
        y_t = dot_rows(p_t, xv[...], NN)
        for i in range(16):
            ymsg[i, :RANK] = y_t[:, TOK * i : TOK * (i + 1)]
            ymsg[i, RANK:] = packed
        yall[own] = ymsg[own]
        flight["yz"] = [
            chain_send(
                ymsg.at[(own + j) % 16], yall.at[own], yz_s.at[j - 1], yz_r.at[j - 1], at_chunk((own + j) % 16)
            )
            for j in range(1, 16)
        ]
        sbuf[6] = jnp.zeros_like(sbuf[6])
        sbuf[7] = jnp.zeros_like(sbuf[7])
        s_t = dot_rows(p_part[...], ev[...], NN)
        for i in range(7):
            width = min(256, HIDDEN - 256 * i)
            sbuf[i, :, :width] = s_t[:, 256 * i : 256 * i + width]

    def right_factor():
        wait_for("yz")
        y_sum = yall[0]
        for i in range(1, 16):
            y_sum = y_sum + yall[i]
        s_t = dot_rows(y_sum[:RANK], gbuf[own], NT)
        for i in range(7):
            width = min(256, HIDDEN - 256 * i)
            sbuf[i, :, :width] += s_t[:, 256 * i : 256 * i + width]
        sin[slot] = sbuf[slot]
        flight["s1"] = [
            chain_send(sbuf.at[(slot + j) % NO], sin.at[slot], s1_s.at[j - 1], s1_r.at[j - 1], at_slot(j))
            for j in range(1, NO)
        ]
        for i in range(4):
            gfull[8 * i : 8 * (i + 1), :RANK] = y_sum[RANK:, RANK * i : RANK * (i + 1)]

    row_id = lax.broadcasted_iota(jnp.int32, (RANK, 128), 0)
    lane_id = lax.broadcasted_iota(jnp.int32, (RANK, 128), 1)

    def eliminate(first, last):
        work = gfull[...]
        if first == 0:
            work = jnp.where(lane_id < RANK, work, jnp.where(lane_id == row_id + RANK, 1.0, 0.0))
        for j in range(first, last):
            ratio = work[:, j : j + 1] / work[j : j + 1, j : j + 1]
            ratio = jnp.where(row_id[:, :1] > j, ratio, 0.0)
            work = work - ratio * work[j : j + 1, :]
        gfull[...] = work

    def scatter_right():
        wait_for("s1")
        total = sin[0]
        for i in range(1, NO):
            total = total + sin[i]
        for i in range(NZ):
            s2[i] = total[8 * (i // 2) : 8 * (i // 2) + 8, 128 * (i % 2) : 128 * (i % 2) + 128]
        s2in[z] = s2[z]
        flight["s2"] = [
            chain_send(s2.at[(z + j) % NZ], s2in.at[z], s2_s.at[j - 1], s2_r.at[j - 1], at_z(j))
            for j in range(1, NZ)
        ]

    def gather_tile():
        wait_for("s2")
        tile = s2in[0]
        for i in range(1, NZ):
            tile = tile + s2in[i]
        s3[z] = tile
        flight["s3"] = [
            chain_send(s3.at[z], s3.at[z], s3_s.at[j - 1], s3_r.at[j - 1], at_z(j)) for j in range(1, NZ)
        ]

    def gather_right():
        wait_for("s3")
        for i in range(NZ):
            s4[slot, 8 * (i // 2) : 8 * (i // 2) + 8, 128 * (i % 2) : 128 * (i % 2) + 128] = s3[i]
        flight["s4"] = [
            chain_send(s4.at[slot], s4.at[slot], s4_s.at[j - 1], s4_r.at[j - 1], at_slot(j)) for j in range(1, NO)
        ]

    def finish_basis():
        work = gfull[...]
        pivots = jnp.sum(jnp.where(lane_id == row_id, work, 0.0), axis=1, keepdims=True)
        gfull[...] = work / jnp.sqrt(pivots)
        p_part[...] = dot_full(gfull[:, RANK : 2 * RANK], p_part[...], NN)

    def approximate():
        wait_for("s4")
        inverse = gfull[:, RANK : 2 * RANK]
        s_all = jnp.concatenate([s4[i] for i in range(7)], axis=1)[:, :HIDDEN]
        second = dot_full(inverse, s_all, NN) * 0.25
        bh, bm, bl = split3(p_part[...])
        qh, qm, ql = split3(second)
        left = jnp.concatenate([bh, bh, bm, bh, bl, bm], axis=0)
        right = jnp.concatenate([qh, qm, qh, ql, qh, qm], axis=0)
        for start in range(0, HIDDEN, 512):
            stop = min(start + 512, HIDDEN)
            block = dot(left, right[:, start:stop], TN)
            abuf[:, start:stop] = block
            macc[:, start:stop] -= block
        upd_out[...] = abuf[my_rows, :].astype(BF16)

    def some(*chunks):
        return lambda: process(*chunks)

    def weights_in():
        for copy in wcopies:
            copy.wait_recv()

    def send_partner_chunk():
        for piece in range(PIECES):
            cross(0, piece).wait_recv()
            ring_send(0, 1, 1, piece)
            ring_send(1, 1, 1, piece)
        issue(0)
        issue(1)

    flight["tz"] = tz
    arrive(1, 0, {})
    arrive(
        2,
        0,
        {
            0: [left_factor],
            1: [weights_in, some(own)],
            2: [some(chunk_of(-1, 0), chunk_of(1, 0))],
            5: [send_partner_chunk, project_tokens],
        },
    )
    arrive(
        3,
        0,
        {0: [some(chunk_of(0, 1))], 2: [some(chunk_of(-2, 0), chunk_of(2, 0))], 5: [right_factor]},
    )
    arrive(
        1,
        1,
        {
            0: [lambda: eliminate(0, 16)],
            1: [lambda: eliminate(16, RANK)],
            2: [some(chunk_of(-3, 0), chunk_of(3, 0))],
            3: [finish_basis],
            4: [scatter_right],
        },
    )
    arrive(4, 0, {0: [some(chunk_of(-1, 1), chunk_of(1, 1))], 2: [some(chunk_of(4, 0))]})
    arrive(2, 1, {1: [gather_tile], 5: [gather_right]})
    process(chunk_of(-2, 1), chunk_of(2, 1))
    cross_wait(1)
    cross_wait(2)
    process(chunk_of(-3, 1), chunk_of(3, 1))
    cross_wait(3)
    process(chunk_of(4, 1))
    approximate()
    err_out[0] = macc[...].astype(BF16)
    advance(0)
    for entry in pending:
        dx_hop(entry[0], 2)

    for copy in sent:
        copy.wait_send()
    for shift in range(NZ):
        for other in range(2):
            chunk = chunk_of(shift, other)

            @pl.when((chunk // 2 - y + NY) % NY != 0)
            def _():
                remote(
                    part.at[chunk], rx.at[chunk], dx_s.at[chunk], dx_r.at[chunk], at_y(1)
                ).wait_send()


def body(activations, cotangent, weight, error_buffer, warm_factor):
    dma = pltpu.SemaphoreType.DMA
    sems = [
        dma((5,)), dma((4 * PIECES,)), dma((4 * PIECES,)), dma((16 * PIECES,)), dma((16 * PIECES,)),
        dma((3,)), dma((3,)), dma((15,)), dma((15,)), dma((3,)), dma((3,)), dma((15,)), dma((15,)),
        dma((7,)), dma((7,)), dma((7,)), dma((7,)), dma((7,)), dma((7,)), dma((7,)), dma((7,)),
        dma((16,)), dma((16 * SUBS,)), dma((16 * SUBS,)),
    ]
    vmem = pltpu.VMEM
    scratch = [
        vmem((16, HIDDEN, TOK), BF16),
        vmem((WIDTH, 16 * TOK), BF16),
        vmem((WIDTH, HIDDEN), BF16),
        vmem((WIDTH, HIDDEN), BF16),
        vmem((RANK, HIDDEN), F32),
        vmem((WIDTH, HIDDEN), F32),
        vmem((WIDTH, HIDDEN), F32),
        vmem((16, WIDTH, TOK), F32),
        vmem((16, WIDTH, TOK), F32),
        vmem((16, WIDTH, TOK), F32),
        vmem((RANK, WIDTH), F32),
        vmem((16, RANK, TOK), F32),
        vmem((4, RANK, WIDTH), F32),
        vmem((8, 128), F32),
        vmem((16, RANK + 8, 128), F32),
        vmem((16, RANK + 8, 128), F32),
        vmem((NO, RANK, 256), F32),
        vmem((NO, RANK, 256), F32),
        vmem((NZ, 8, 128), F32),
        vmem((NZ, 8, 128), F32),
        vmem((NZ, 8, 128), F32),
        vmem((NO, RANK, 256), F32),
        vmem((RANK, 128), F32),
    ]
    hbm = pl.BlockSpec(memory_space=pltpu.HBM)
    vspec = pl.BlockSpec(memory_space=pltpu.VMEM)
    gradient_t, error_next, update = pl.pallas_call(
        kernel,
        out_shape=(
            jax.ShapeDtypeStruct((1, WIDTH, 2 * TOK), BF16),
            jax.ShapeDtypeStruct((1, WIDTH, HIDDEN), BF16),
            jax.ShapeDtypeStruct((ROWS, HIDDEN), BF16),
        ),
        in_specs=[hbm] * 5,
        out_specs=(vspec, vspec, vspec),
        scratch_shapes=scratch + sems,
        compiler_params=pltpu.CompilerParams(
            collective_id=0, has_side_effects=True, vmem_limit_bytes=60 * 1024 * 1024
        ),
        cost_estimate=pl.CostEstimate(flops=4600000000, bytes_accessed=8000000, transcendentals=0),
    )(
        jnp.swapaxes(activations, 1, 2), jnp.swapaxes(cotangent, 1, 2), weight, error_buffer, warm_factor.T
    )
    return jnp.swapaxes(gradient_t, 1, 2), error_next, update


def solution(mesh):
    in_specs = (
        P("dp", None, None),
        P("dp", None, "tensor"),
        P("dp", "tensor"),
        P("dp", None, "tensor"),
        P("tensor", None),
    )
    out_specs = (P("dp", "tensor", None), P("dp", None, "tensor"), P("dp", "tensor"))
    return jax.shard_map(body, mesh=mesh, in_specs=in_specs, out_specs=out_specs, check_vma=False)
```

time: 732 us -> 127 us (0.17)
  the two profiles are of different devices: /device:TPU:40 before, /device:TPU:24 now
where the time goes in v2:
time: 127 us; the launch traced here: 126 us
  Pallas kernels  121 us (95%)
  local copies, waits for them, and re-layouts  4.69 us (4%)
    pallas_call x1, Pallas kernels, body(): pl.pallas_call(kernel, out_shape=(jax.ShapeDtypeStruct((1, WIDTH, 2 * TOK...  121 us
    unnamed x5, local copies, waits for them, and re-layouts  4.69 us

profile of v2, /device:TPU:24, one launch (start us, length us, event | category | flops | bytes accessed | tf_op | source)
XLA Modules:
  0.0 126.4 jit_solution(17731626866769411689)
XLA Ops:
  0.6 121.1 %shard_map.76 = (bf16[1,320,256]{2,1,0:T(8,128)(2,1)}, bf16[1,320,1728]{2,1,0:T(8,128)(2,1)}, bf16[80,1728]{1,0:T(8,128)(2,1)}) custom-call(bf16[1,320,2048]{2,1,0:T(8,128)(2,1)} %bitcast.5, bf16[1,1728,128]{2,1,0:T(8,128)(2,1)} %bitcast.6, bf16[80,1728]{1,0:T(8,128)(2,1)} %w_hbm.1, bf16[1,320,1728]{2,1,0:T(8,128)(2,1)} %e_hbm.1, f32[32,1728]{1,0:T(8,128)} %bitcast.7), custom_call_target="tpu_custom_call" | custom-call | flops 4600000000 | bytes 8000000 | tf_op jit(solution)/shard_map/pallas_call | solution.py:532
  121.7 1.6 %copy.11 = bf16[1,256,320]{1,2,0:T(8,128)(2,1)} copy(bf16[1,256,320]{1,2,0:T(8,128)(2,1)} %bitcast.4) | data formatting | bytes 327680
  123.3 0.0 copy-start
  123.3 2.4 %copy.12 = bf16[1,320,1728]{2,1,0:T(8,128)(2,1)} copy(bf16[1,320,1728]{2,1,0:T(8,128)(2,1)} %get-tuple-element.13) | data formatting | bytes 2211840
  125.7 0.0 copy-done
  125.7 0.7 copy.13
Async XLA Ops:
  123.3 2.4 %copy-start = (bf16[80,1728]{1,0:T(8,128)(2,1)S(1)}, bf16[80,1728]{1,0:T(8,128)(2,1)}, u32[]{:S(2)}) copy-start(bf16[80,1728]{1,0:T(8,128)(2,1)} %get-tuple-element.14) | copy-start | bytes 829444

commit v3 on v2

--- a/solution.py
+++ b/solution.py
@@ -19,7 +19,7 @@
 PIECES = 6
 PIECE = HIDDEN // PIECES
 SUBS = 4
-SPACING = 8
+SPACING = 5
 DEPTH = 4
 SUB = WIDTH // SUBS
 NN = (((1,), (0,)), ((), ()))
@@ -232,32 +232,34 @@
                 {"dp": me, "tensor": root},
             )
 
+        def pass_on(copy):
+            for sub in range(SUBS):
+                near(sub, turn).wait_recv()
+                rows = pl.ds(sub * SUB, SUB)
+                part[chunk, rows] += rx[chunk, rows]
+                copy(sub).start()
+
         if stage == 0:
 
-            @pl.when((d == 4) | (d == 2))
+            @pl.when((d == 4) | (d == 5))
             def _():
+                step = jnp.where(d == 4, turn, -turn)
                 for sub in range(SUBS):
-                    near(sub, turn).start()
-
-            @pl.when(d == 5)
+                    near(sub, step).start()
+
+        elif stage == 1:
+
+            @pl.when((d == 3) | (d == 6))
             def _():
-                for sub in range(SUBS):
-                    near(sub, -turn).start()
-
-            @pl.when(d == 7)
-            def _():
-                for sub in range(SUBS):
-                    last(sub, d).start()
-
-        elif stage == 1:
-
-            @pl.when((d == 1) | (d == 3) | (d == 6))
-            def _():
-                for sub in range(SUBS):
-                    near(sub, turn).wait_recv()
-                    rows = pl.ds(sub * SUB, SUB)
-                    part[chunk, rows] += rx[chunk, rows]
-                    last(sub, d).start()
+                step = jnp.where(d == 3, turn, -turn)
+                pass_on(lambda sub: near(sub, step))
+
+        elif stage == 2:
+            pl.when(d == 2)(lambda: pass_on(lambda sub: near(sub, turn)))
+            pl.when(d == 7)(lambda: pass_on(lambda sub: last(sub, d)))
+
+        elif stage == 3:
+            pl.when(d == 1)(lambda: pass_on(lambda sub: last(sub, d)))
 
         else:
 
@@ -267,7 +269,7 @@
                 for sub in range(SUBS):
                     rows = pl.ds(sub * SUB, SUB)
                     total = part[chunk, rows]
-                    for distance in (7, 1, 6, 3):
+                    for distance in (7, 1):
                         arrived = remote(
                             part.at[chunk, rows], rxb.at[chunk % 2 * NY + distance, rows], dx_s.at[chunk],
                             dxb_r.at[(chunk % 2 * NY + distance) * SUBS + sub], at_y(1),
@@ -280,7 +282,7 @@
 
     def advance(spacing=SPACING):
         clock[0] += 1
-        for stage in (1,):
+        for stage in (3, 2, 1):
             for entry in pending:
                 if entry[1] == stage and clock[0] - entry[2] >= spacing:
                     dx_hop(entry[0], stage)
@@ -294,11 +296,11 @@
 
     def process(*chunks):
         for chunk in chunks:
-            accumulate(chunk)
-        for chunk in chunks:
             part[chunk] = dot(wslab[...], gbuf[chunk], NN)
             dx_hop(chunk, 0)
             pending.append([chunk, 1, clock[0]])
+        for chunk in chunks:
+            accumulate(chunk)
 
     flight = {}
 
@@ -447,38 +449,42 @@
             0: [left_factor],
             1: [weights_in, some(own)],
             2: [some(chunk_of(-1, 0), chunk_of(1, 0))],
-            5: [send_partner_chunk, project_tokens],
+            5: [send_partner_chunk],
         },
     )
     arrive(
         3,
         0,
-        {0: [some(chunk_of(0, 1))], 2: [some(chunk_of(-2, 0), chunk_of(2, 0))], 5: [right_factor]},
+        {0: [some(chunk_of(0, 1))], 1: [project_tokens], 2: [some(chunk_of(-2, 0), chunk_of(2, 0))]},
     )
     arrive(
         1,
         1,
         {
-            0: [lambda: eliminate(0, 16)],
-            1: [lambda: eliminate(16, RANK)],
-            2: [some(chunk_of(-3, 0), chunk_of(3, 0))],
-            3: [finish_basis],
-            4: [scatter_right],
+            0: [some(chunk_of(-3, 0), chunk_of(3, 0))],
+            2: [right_factor],
+            4: [lambda: eliminate(0, 16)],
+            5: [lambda: eliminate(16, RANK)],
         },
     )
     arrive(4, 0, {0: [some(chunk_of(-1, 1), chunk_of(1, 1))], 2: [some(chunk_of(4, 0))]})
-    arrive(2, 1, {1: [gather_tile], 5: [gather_right]})
-    process(chunk_of(-2, 1), chunk_of(2, 1))
+    arrive(2, 1, {0: [scatter_right], 2: [finish_basis]})
     cross_wait(1)
     cross_wait(2)
-    process(chunk_of(-3, 1), chunk_of(3, 1))
+    process(chunk_of(-2, 1), chunk_of(2, 1), chunk_of(-3, 1), chunk_of(3, 1))
+    advance(3)
     cross_wait(3)
     process(chunk_of(4, 1))
+    gather_tile()
+    advance(1)
+    gather_right()
+    advance(0)
     approximate()
     err_out[0] = macc[...].astype(BF16)
     advance(0)
+    advance(0)
     for entry in pending:
-        dx_hop(entry[0], 2)
+        dx_hop(entry[0], 4)
 
     for copy in sent:
         copy.wait_send()

time: 127 us -> 117 us (0.921)
  the two profiles are of different devices: /device:TPU:24 before, /device:TPU:16 now
where the time goes in v3:
time: 117 us
  Pallas kernels  112 us (96%)
  local copies, waits for them, and re-layouts  4.69 us (4%)
    pallas_call x1, Pallas kernels, body(): pl.pallas_call(kernel, out_shape=(jax.ShapeDtypeStruct((1, WIDTH, 2 * TOK...  112 us
    unnamed x5, local copies, waits for them, and re-layouts  4.69 us

profile of v3, /device:TPU:16, one launch (start us, length us, event | category | flops | bytes accessed | tf_op | source)
XLA Modules:
  0.0 116.9 jit_solution(7547539321144701724)
XLA Ops:
  0.6 111.6 %shard_map.76 = (bf16[1,320,256]{2,1,0:T(8,128)(2,1)}, bf16[1,320,1728]{2,1,0:T(8,128)(2,1)}, bf16[80,1728]{1,0:T(8,128)(2,1)}) custom-call(bf16[1,320,2048]{2,1,0:T(8,128)(2,1)} %bitcast.5, bf16[1,1728,128]{2,1,0:T(8,128)(2,1)} %bitcast.6, bf16[80,1728]{1,0:T(8,128)(2,1)} %w_hbm.1, bf16[1,320,1728]{2,1,0:T(8,128)(2,1)} %e_hbm.1, f32[32,1728]{1,0:T(8,128)} %bitcast.7), custom_call_target="tpu_custom_call" | custom-call | flops 4600000000 | bytes 8000000 | tf_op jit(solution)/shard_map/pallas_call | solution.py:538
  112.2 1.6 %copy.11 = bf16[1,256,320]{1,2,0:T(8,128)(2,1)} copy(bf16[1,256,320]{1,2,0:T(8,128)(2,1)} %bitcast.4) | data formatting | bytes 327680
  113.8 0.0 copy-start
  113.8 2.4 %copy.12 = bf16[1,320,1728]{2,1,0:T(8,128)(2,1)} copy(bf16[1,320,1728]{2,1,0:T(8,128)(2,1)} %get-tuple-element.13) | data formatting | bytes 2211840
  116.2 0.0 copy-done
  116.2 0.7 copy.13
Async XLA Ops:
  113.8 2.4 %copy-start = (bf16[80,1728]{1,0:T(8,128)(2,1)S(1)}, bf16[80,1728]{1,0:T(8,128)(2,1)}, u32[]{:S(2)}) copy-start(bf16[80,1728]{1,0:T(8,128)(2,1)} %get-tuple-element.14) | copy-start | bytes 829444
